TPU v7x, 32 devices: a whole 2x2x4 slice. The times are simulated.
32 devices in a mesh: groups: 1, tensor: 32 (over z, y, x, core), dp: 1.
Axes of the slice: x: 2, y: 2, z: 4, core: 2. Of those that a mesh axis runs over, the one named last changes fastest.
Arguments:
- layer_input: bfloat16 [256, 8192], P(('groups', 'dp'), 'tensor'), may hold values from -180 to 180
- out_grad: bfloat16 [256, 8192], P(('groups', 'dp'), 'tensor'), may hold values from -6 to 6
- norm_gain: float32 [8192], replicated, may hold values from 0.25 to 1.75
- w_gate: bfloat16 [8192, 3584], P('dp', 'tensor'), may hold values from -0.0625 to 0.0625
- w_up: bfloat16 [8192, 3584], P('dp', 'tensor'), may hold values from -0.0625 to 0.0625
- w_down: bfloat16 [3584, 8192], P('tensor', 'dp'), may hold values from -0.09375 to 0.09375
- pin_gate: bfloat16 [8192, 64], P('tensor'), may hold values from -0.0625 to 0.0625
- pin_up: bfloat16 [8192, 64], P('tensor'), may hold values from -0.0625 to 0.0625
- pout_gate: bfloat16 [3584, 64], P('tensor'), may hold values from -0.09375 to 0.09375
- pout_up: bfloat16 [3584, 64], P('tensor'), may hold values from -0.09375 to 0.09375
- pin_down: bfloat16 [3584, 64], P('tensor'), may hold values from -0.09375 to 0.09375
- pout_down: bfloat16 [8192, 64], P('tensor'), may hold values from -0.0625 to 0.0625
- targets: float32 [1024, 12288], P('tensor'), may hold values from -0.0546875 to 0.0546875
Outputs:
- features: float32 [4, 12288], P(('groups', 'dp'))
- scores: float32 [4, 1024], P(('groups', 'dp'), 'tensor')
All inputs are finite; a program needn't handle non-finite values.
Results may differ from a plain program's by a relative error of at most 0.0052.
Values may be sent and summed in bfloat16 or wider, within the bound.
A program may use at most 64 MiB of HBM per device.

v0:
```python
import jax
import jax.numpy as jnp
from jax import lax
from jax.sharding import PartitionSpec as P

SEQ = 64


EPSILON = 1e-05


def project_pair(out_side, in_side):
    out_rows = out_side.reshape(-1, SEQ, out_side.shape[-1])
    in_rows = in_side.reshape(-1, SEQ, in_side.shape[-1])
    product = jnp.einsum("esi,esj->eij", out_rows, in_rows, precision=lax.Precision.HIGHEST)
    return product.reshape(product.shape[0], -1)


def on_device(
    layer_input,
    out_grad,
    norm_gain,
    w_gate,
    w_up,
    w_down,
    pin_gate,
    pin_up,
    pout_gate,
    pout_up,
    pin_down,
    pout_down,
    targets,
):
    shard_width = layer_input.shape[1]
    first_col = lax.axis_index("tensor") * shard_width
    gathered = lax.all_gather(layer_input, "tensor", axis=1, tiled=True)
    wide_rows = gathered.astype(jnp.float32)
    mean_square = jnp.mean(wide_rows * wide_rows, axis=-1, keepdims=True)
    normed = (wide_rows * lax.rsqrt(mean_square + EPSILON) * norm_gain).astype(jnp.bfloat16)
    normed_piece = lax.dynamic_slice_in_dim(normed, first_col, shard_width, 1)
    columns = normed
    gate_pre = jnp.dot(
        columns,
        lax.all_gather(w_gate, "dp", axis=0, tiled=True),
        preferred_element_type=jnp.float32,
    )
    up_pre = jnp.dot(
        columns, lax.all_gather(w_up, "dp", axis=0, tiled=True), preferred_element_type=jnp.float32
    )
    sigmoid_gate = jax.nn.sigmoid(gate_pre)
    activated = gate_pre * sigmoid_gate
    hidden_act = (activated * up_pre).astype(jnp.bfloat16)
    a_gate_part = jnp.dot(normed_piece, pin_gate, preferred_element_type=jnp.float32)
    a_up_part = jnp.dot(normed_piece, pin_up, preferred_element_type=jnp.float32)
    b_down_part = jnp.dot(out_grad, pout_down, preferred_element_type=jnp.float32)
    grad_rows = lax.all_gather(out_grad, "tensor", axis=1, tiled=True)
    columns = grad_rows
    grad_hidden = jnp.einsum(
        "td,hd->th",
        columns,
        lax.all_gather(w_down, "dp", axis=1, tiled=True),
        preferred_element_type=jnp.float32,
    )
    grad_gate = (
        grad_hidden * up_pre * sigmoid_gate * (1.0 + gate_pre * (1.0 - sigmoid_gate))
    ).astype(jnp.bfloat16)
    grad_up = (grad_hidden * activated).astype(jnp.bfloat16)
    b_gate_part = jnp.dot(grad_gate, pout_gate, preferred_element_type=jnp.float32)
    b_up_part = jnp.dot(grad_up, pout_up, preferred_element_type=jnp.float32)
    a_down_part = jnp.dot(hidden_act, pin_down, preferred_element_type=jnp.float32)
    a_gate, a_up, b_down, b_gate, b_up, a_down = lax.psum(
        (a_gate_part, a_up_part, b_down_part, b_gate_part, b_up_part, a_down_part), "tensor"
    )
    features = jnp.concatenate(
        [project_pair(b_gate, a_gate), project_pair(b_up, a_up), project_pair(b_down, a_down)],
        axis=1,
    )
    scores = jnp.dot(
        features, targets.T, precision=lax.Precision.HIGHEST, preferred_element_type=jnp.float32
    )
    return (features, scores)


def solution(mesh):
    return jax.shard_map(
        on_device,
        mesh=mesh,
        in_specs=(
            P(("groups", "dp"), "tensor"),
            P(("groups", "dp"), "tensor"),
            P(),
            P("dp", "tensor"),
            P("dp", "tensor"),
            P("tensor", "dp"),
            P("tensor", None),
            P("tensor", None),
            P("tensor", None),
            P("tensor", None),
            P("tensor", None),
            P("tensor", None),
            P("tensor", None),
        ),
        out_specs=(P(("groups", "dp"), None), P(("groups", "dp"), "tensor")),
        check_vma=False,
    )
```

profile of v0, /device:TPU:1, one launch (start us, length us, event | category | flops | bytes accessed | tf_op | source)
XLA Modules:
  0.0 314.5 jit_solution(17929270182736945570)
XLA Ops:
  7.2 0.0 copy-start
  7.2 0.0 copy-start.6
  7.2 0.0 all-gather.5.cloned.1.call-start
  7.2 0.7 all-gather.5.cloned.1.call-update
  7.9 0.0 all-gather.3.cloned.1.call-start
  8.0 0.7 all-gather.3.cloned.1.call-update
  8.7 0.0 all-reduce.3.cloned.1.call-start
  8.7 1.1 fusion.23
  9.8 0.1 reshape.46
  9.9 0.7 copy.19
  10.6 69.4 %all-gather.5.cloned.1.call-done = bf16[256,8192]{1,0:T(8,128)(2,1)} async-done(((bf16[256,256]{1,0:T(8,128)(2,1)}), bf16[256,8192]{1,0:T(8,128)(2,1)}) %all-gather.5.cloned.1.call-update) | async-done | bytes 4194320 | tf_op jit(solution)/shard_map/all_gather | solution.py:36
  79.9 0.0 copy-start.2
  79.9 3.3 %fusion = f32[256]{0:T(256)S(1)} fusion(bf16[256,8192]{1,0:T(8,128)(2,1)} %all-gather.5.cloned.1.call-done), kind=kLoop, calls=%fused_computation.2 | loop fusion | flops 6291200 | bytes 4195328 | tf_op jit(solution)/shard_map/reduce_sum | solution.py:38
  83.2 0.0 copy-done.6
  83.2 0.2 copy-done.2
  83.4 1.2 fusion.2
  84.6 0.0 copy-start.1
  84.6 1.9 copy-done.1
  86.5 0.0 copy-done
  86.5 1.5 fusion.20
  88.0 0.0 copy-start.7
  88.1 60.4 %all-gather.3.cloned.1.call-done = bf16[256,8192]{1,0:T(8,128)(2,1)} async-done(((bf16[256,256]{1,0:T(8,128)(2,1)}), bf16[256,8192]{1,0:T(8,128)(2,1)}) %all-gather.3.cloned.1.call-update) | async-done | bytes 4194320 | tf_op jit(solution)/shard_map/all_gather | solution.py:56
  148.4 4.3 %fusion.18 = f32[256,112]{0,1:T(8,128)S(1)} fusion(bf16[256,8192]{1,0:T(8,128)(2,1)} %all-gather.3.cloned.1.call-done, bf16[112,8192]{1,0:T(8,128)(2,1)} %param.18), kind=kOutput, calls=%fused_computation.26 | convolution fusion | flops 469762048 | bytes 6144000 | tf_op jit(solution)/shard_map/td,hd->th/dot_general | solution.py:58
  152.7 0.0 copy-start.4
  152.7 0.6 copy-done.4
  153.3 0.0 copy-done.7
  153.3 0.0 copy-start.8
  153.3 0.0 copy-start.9
  153.3 0.2 fusion.8
  153.5 0.1 reshape.43
  153.6 0.0 copy-start.5
  153.6 0.7 copy.17
  154.3 0.0 copy-start.3
  154.3 4.4 %fusion.19 = f32[256,112]{0,1:T(8,128)S(1)} fusion(bf16[256,8192]{1,0:T(8,128)(2,1)} %copy-done.1, bf16[8192,112]{0,1:T(8,128)(2,1)} %param.17), kind=kOutput, calls=%fused_computation.27 | convolution fusion | flops 469762048 | bytes 6144000 | tf_op jit(solution)/shard_map/dot_general | solution.py:47
  158.7 0.0 copy-done.8
  158.7 0.0 copy-done.5
  158.7 0.8 fusion.10
  159.5 0.0 copy-done.9
  159.5 0.9 fusion.9
  160.4 0.9 reshape.40
  161.3 0.7 copy.15
  162.0 1.7 fusion.3
  163.7 1.7 fusion.5
  165.5 0.0 all-reduce.3.cloned.1.call-update
  165.5 129.4 %all-reduce.3.cloned.1.call-done = (f32[4,64,64]{1,2,0:T(8,128)}, f32[4,64,64]{2,1,0:T(8,128)}, f32[4,64,64]{1,2,0:T(8,128)}, f32[4,64,64]{2,1,0:T(8,128)}, f32[4,64,64]{1,2,0:T(8,128)}, /*index=5*/f32[4,64,64]{2,1,0:T(8,128)}) async-done(((f32[4,64,64]{1,2,0:T(8,128)}, f32[4,64,64]{2,1,0:T(8,128)}, f32[4,64,64]{1,2,0:T(8,128)}, f32[4,64,64]{2,1,0:T(8,128)}, f32[4,64,64]{1,2,0:T(8,128)}, ...) | async-done | bytes 393232 | tf_op jit(solution)/shard_map/psum | solution.py:71
  294.9 1.2 fusion.21
  296.1 0.7 reshape.42
  296.8 1.5 constant_dynamic-update-slice_fusion.2
  298.3 1.2 fusion.22
  299.5 0.7 reshape.45
  300.3 1.2 fusion.24
  301.5 0.7 reshape.48
  302.2 1.5 constant_dynamic-update-slice_fusion.1
  303.7 1.5 constant_dynamic-update-slice_fusion
  305.2 0.0 copy-done.3
  305.2 2.8 fusion.25
  (1 shorter events, 0.0 us)
Async XLA Ops:
  7.2 79.4 %copy-start = (bf16[8192,112]{0,1:T(8,128)(2,1)S(1)}, bf16[8192,112]{0,1:T(8,128)(2,1)}, u32[]{:S(2)}) copy-start(bf16[8192,112]{0,1:T(8,128)(2,1)} %param.16) | copy-start | bytes 5505028
  7.2 76.0 %copy-start.6 = (f32[8192]{0:T(1024)S(1)}, f32[8192]{0:T(1024)}, u32[]{:S(2)}) copy-start(f32[8192]{0:T(1024)} %param.15) | copy-start | bytes 98308
  7.2 72.8 %all-gather.5.cloned.1.call-start = ((), (), s32[]{:S(2)}) async-start(), calls=%async_computation.1 | async-start | bytes 4325376 | tf_op jit(solution)/shard_map/all_gather | solution.py:36
  7.9 140.5 %all-gather.3.cloned.1.call-start = ((), (), s32[]{:S(2)}) async-start(), calls=%async_computation | async-start | bytes 4325376 | tf_op jit(solution)/shard_map/all_gather | solution.py:56
  8.7 286.2 %all-reduce.3.cloned.1.call-start = ((), (), s32[]{:S(2)}) async-start(), calls=%async_computation.2 | async-start | bytes 1572864 | tf_op jit(solution)/shard_map/psum | solution.py:71
  79.9 3.4 %copy-start.2 = (bf16[256,8192]{1,0:T(8,128)(2,1)S(1)}, bf16[256,8192]{1,0:T(8,128)(2,1)}, u32[]{:S(2)}) copy-start(bf16[256,8192]{1,0:T(8,128)(2,1)} %all-gather.5.cloned.1.call-done) | copy-start | bytes 12582916
  84.6 2.0 copy-start.1
  88.0 65.3 %copy-start.7 = (bf16[112,64]{0,1:T(8,128)(2,1)S(1)}, bf16[112,64]{0,1:T(8,128)(2,1)}, u32[]{:S(2)}) copy-start(bf16[112,64]{0,1:T(8,128)(2,1)} %param.22) | copy-start | bytes 43012
  152.7 0.6 copy-start.4
  153.3 5.3 %copy-start.8 = (bf16[112,64]{0,1:T(8,128)(2,1)S(1)}, bf16[112,64]{0,1:T(8,128)(2,1)}, u32[]{:S(2)}) copy-start(bf16[112,64]{0,1:T(8,128)(2,1)} %param.21) | copy-start | bytes 43012
  153.3 6.2 %copy-start.9 = (bf16[112,64]{0,1:T(8,128)(2,1)S(1)}, bf16[112,64]{0,1:T(8,128)(2,1)}, u32[]{:S(2)}) copy-start(bf16[112,64]{0,1:T(8,128)(2,1)} %param.23) | copy-start | bytes 43012
  153.6 5.1 %copy-start.5 = (f32[256,112]{0,1:T(8,128)S(1)}, f32[256,112]{0,1:T(8,128)}, u32[]{:S(2)}) copy-start(f32[256,112]{0,1:T(8,128)} %copy-done.4) | copy-start | bytes 344068
  154.3 150.9 %copy-start.3 = (f32[32,12288]{1,0:T(8,128)S(1)}, f32[32,12288]{1,0:T(8,128)}, u32[]{:S(2)}) copy-start(f32[32,12288]{1,0:T(8,128)} %param.25) | copy-start | bytes 4718596
Sparse Core Ops, SparseCore 0:
  10.9 68.9 all-gather.4
  82.8 65.5 all-gather.2
  165.6 129.2 all-reduce.2
where the time goes:
time: 316 us; the launch traced here: 315 us
  waiting for transfers between devices  261 us (83%)
  matrix products  23 us (7%)
  between operations  13.9 us (4%)
  local copies, waits for them, and re-layouts  12.6 us (4%)
  other arithmetic  4.45 us (1%)
    psum x1, waiting for transfers between devices, on_device(): lax.psum((a_gate_part, a_up_part, b_down_part, b_gate_part, b_up_part, a_...  129 us
    all_gather x1, waiting for transfers between devices, on_device(): gathered = lax.all_gather(layer_input, 'tensor', axis=1, tiled=True)  69.4 us
    all_gather x1, waiting for transfers between devices, on_device(): grad_rows = lax.all_gather(out_grad, 'tensor', axis=1, tiled=True)  60.4 us
  transfers between devices with their start and end apart: 3, of which 3 were waited for; matrix products, arithmetic and copies ran while one was open for 2% of the time, Pallas kernels for 0%

commit v1 on v0

--- a/solution.py
+++ b/solution.py
@@ -1,12 +1,366 @@
+import functools
 import jax
 import jax.numpy as jnp
 from jax import lax
+from jax.experimental import pallas as pl
+from jax.experimental.pallas import tpu as pltpu
 from jax.sharding import PartitionSpec as P
 
 SEQ = 64
 
 
 EPSILON = 1e-05
+F32 = jnp.float32
+BF16 = jnp.bfloat16
+CHIPS = 16
+PAD = 128
+
+
+def dot_nt(a, b):
+    return lax.dot_general(a, b, (((1,), (1,)), ((), ())), preferred_element_type=F32)
+
+
+def kernel(
+    x_ref, g_ref, gain_ref, wg_hbm, wu_hbm, wd_hbm, pg_ref, pu_ref, qg_ref, qu_ref, pd_ref, qd_ref,
+    out_ref,
+    buf, wgu, wd, ss, gu_acc, h_acc, part, pair, own, rs,
+    recv, send, w_sem, pair_sem, rs_send, rs_recv, ag_send, ag_recv, sib_send, sib_recv,
+):
+    me = lax.axis_index("tensor")
+    z, y, x, c = me // 8, (me // 4) % 2, (me // 2) % 2, me % 2
+    chip = me // 2
+    sib = me + 1 - 2 * c
+    width = x_ref.shape[1]
+    tokens = x_ref.shape[0]
+    half = tokens // 2
+    hid = wg_hbm.shape[0]
+
+    loads = [
+        pltpu.make_async_copy(wg_hbm, wgu.at[pl.ds(0, hid)], w_sem.at[0]),
+        pltpu.make_async_copy(wu_hbm, wgu.at[pl.ds(PAD, hid)], w_sem.at[1]),
+        pltpu.make_async_copy(wd_hbm, wd, w_sem.at[2]),
+    ]
+    for load in loads:
+        load.start()
+
+    barrier = pltpu.get_barrier_semaphore()
+
+    @pl.loop(1, CHIPS)
+    def _(i):
+        peer = ((chip + i) % CHIPS) * 2 + c
+        pl.semaphore_signal(barrier, inc=1, device_id={"tensor": peer})
+
+    pl.semaphore_signal(barrier, inc=1, device_id={"tensor": sib})
+    buf[0, me] = x_ref[...]
+    buf[1, me] = g_ref[...]
+    pl.semaphore_wait(barrier, CHIPS)
+
+    def dev(zz, fy, fx, cc):
+        yy = 1 - y if fy else y
+        xx = 1 - x if fx else x
+        return ((zz * 2 + yy) * 2 + xx) * 2 + cc
+
+    order = [
+        z,
+        jnp.where(z == 0, 1, z - 1),
+        jnp.where(z == 0, 2, jnp.where(z == 3, 1, z + 1)),
+        jnp.where(z < 2, 3, 0),
+    ]
+    counter = [0]
+    pending = []
+
+    def copy(a, h, owner, to, slot):
+        block = buf.at[a, owner, pl.ds(h * half, half)]
+        return pltpu.make_async_remote_copy(
+            src_ref=block, dst_ref=block,
+            send_sem=send.at[slot], recv_sem=recv.at[(a * 2 + h) * 32 + owner],
+            device_id={"tensor": to},
+        )
+
+    def start(a, h, owner, to, cond=None):
+        slot = counter[0]
+        counter[0] += 1
+        if cond is None:
+            copy(a, h, owner, to, slot).start()
+        else:
+            @pl.when(cond)
+            def _():
+                copy(a, h, owner, to, slot).start()
+        pending.append((a, h, owner, to, slot, cond))
+
+    def arrive(a, h, owner):
+        copy(a, h, owner, sib, 0).wait_recv()
+
+    def flips(h, stage):
+        if stage == 0:
+            return [(0, 0)]
+        if stage == 1:
+            return [(0, 1)] if h == 0 else [(1, 0)]
+        return [(1, 0), (1, 1)] if h == 0 else [(0, 1), (1, 1)]
+
+    def lane_event(a, stage, k):
+        for h in (0, 1):
+            for fy, fx in flips(h, stage):
+                owner = dev(order[k], fy, fx, c)
+                if not (stage == 0 and k == 0):
+                    arrive(a, h, owner)
+                n1 = dev(z, 0, 1, c) if h == 0 else dev(z, 1, 0, c)
+                n2 = dev(z, 1, 0, c) if h == 0 else dev(z, 0, 1, c)
+                if stage == 0:
+                    if k == 0:
+                        start(a, h, owner, me + 8, z < 3)
+                        start(a, h, owner, me - 8, z > 0)
+                    elif k < 3:
+                        up = order[k] < z
+                        start(a, h, owner, jnp.where(up, me + 8, me - 8),
+                              jnp.logical_or(jnp.logical_and(up, z < 3),
+                                             jnp.logical_and(order[k] > z, z > 0)))
+                    else:
+                        up = order[k] < z
+                        start(a, h, owner, jnp.where(up, me + 8, me - 8),
+                              jnp.logical_or(jnp.logical_and(up, z < 3),
+                                             jnp.logical_and(order[k] > z, z > 0)))
+                    start(a, h, owner, n1)
+                if stage < 2:
+                    start(a, h, owner, n2)
+                start(a, h, owner, sib)
+
+    def sib_event(a, k):
+        for h in (0, 1):
+            for fy in (0, 1):
+                for fx in (0, 1):
+                    arrive(a, h, dev(order[k], fy, fx, 1 - c))
+
+    def owner_of(k, i, cc):
+        return (order[k] * 4 + i) * 2 + cc
+
+    def squares(k, cc):
+        @pl.loop(0, 4)
+        def _(i):
+            v = buf[0, owner_of(k, i, cc)].astype(F32)
+            v = v * v
+            ss[...] += v[:, :128] + v[:, 128:]
+
+    def grads(k, cc):
+        @pl.loop(0, 4)
+        def _(i):
+            owner = owner_of(k, i, cc)
+            cols = pl.ds(pl.multiple_of(owner * width, width), width)
+            h_acc[...] += dot_nt(buf[1, owner], wd[:, cols])
+
+    def tick(a, t):
+        work = squares if a == 0 else grads
+        for stage in (0, 1, 2):
+            k = t - stage
+            if 0 <= k < 4:
+                lane_event(a, stage, k)
+        k = t - 2
+        if 0 <= k < 4:
+            work(k, c)
+        k = t - 3
+        if 0 <= k < 4:
+            sib_event(a, k)
+            work(k, 1 - c)
+
+    def normed_of(owner):
+        cols = pl.ds(pl.multiple_of(owner * width, width), width)
+        scale = ss[:, 0:1]
+        return (buf[0, owner].astype(F32) * scale * gain_ref[:, cols]).astype(BF16), cols
+
+    def pre(lo, hi):
+        @pl.loop(lo, hi)
+        def _(owner):
+            normed, cols = normed_of(owner)
+            gu_acc[...] += dot_nt(normed, wgu[:, cols])
+
+    ss[...] = jnp.zeros_like(ss)
+    gu_acc[...] = jnp.zeros_like(gu_acc)
+    h_acc[...] = jnp.zeros_like(h_acc)
+    wgu[pl.ds(hid, PAD - hid)] = jnp.zeros((PAD - hid, wgu.shape[1]), BF16)
+    wgu[pl.ds(PAD + hid, PAD - hid)] = jnp.zeros((PAD - hid, wgu.shape[1]), BF16)
+    for t in (0, 1, 2, 3):
+        tick(0, t)
+        if t == 2:
+            for load in loads:
+                load.wait()
+    tick(1, 0)
+    tick(0, 4)
+    tick(1, 1)
+    tick(0, 5)
+    tick(1, 2)
+    tick(0, 6)
+    total = jnp.sum(ss[...], axis=1, keepdims=True)
+    ss[...] = jnp.broadcast_to(lax.rsqrt(total / (32 * width) + EPSILON), ss.shape)
+    rank = pg_ref.shape[0]
+    tick(1, 3)
+    pre(0, 12)
+    tick(1, 4)
+    pre(12, 24)
+    tick(1, 5)
+    pre(24, 32)
+    mine, _ = normed_of(me)
+    part[:, 0:rank] = dot_nt(mine, pg_ref[...])
+    part[:, rank:2 * rank] = dot_nt(mine, pu_ref[...])
+    part[:, 2 * rank:3 * rank] = dot_nt(g_ref[...], qd_ref[...])
+    gate_pre = gu_acc[:, 0:hid]
+    up_pre = gu_acc[:, PAD:PAD + hid]
+    sigmoid_gate = jax.nn.sigmoid(gate_pre)
+    activated = gate_pre * sigmoid_gate
+    hidden_act = (activated * up_pre).astype(BF16)
+    part[:, 5 * rank:6 * rank] = dot_nt(hidden_act, pd_ref[...])
+    tick(1, 6)
+    grad_hidden = h_acc[...]
+    grad_gate = (
+        grad_hidden * up_pre * sigmoid_gate * (1.0 + gate_pre * (1.0 - sigmoid_gate))
+    ).astype(BF16)
+    grad_up = (grad_hidden * activated).astype(BF16)
+    part[:, 3 * rank:4 * rank] = dot_nt(grad_gate, qg_ref[...])
+    part[:, 4 * rank:5 * rank] = dot_nt(grad_up, qu_ref[...])
+
+    swap = pltpu.make_async_remote_copy(
+        src_ref=part.at[pl.ds(pl.multiple_of((1 - c) * half, half), half)], dst_ref=pair,
+        send_sem=pair_sem.at[0], recv_sem=pair_sem.at[1], device_id={"tensor": sib},
+    )
+    swap.start()
+    rows = half // CHIPS
+    swap.wait_recv()
+    own[...] = part[pl.ds(pl.multiple_of(c * half, half), half)] + pair[...]
+
+    def scatter(i, to_me):
+        j = (chip + i) % CHIPS
+        slot = (chip + CHIPS - i) % CHIPS
+        return pltpu.make_async_remote_copy(
+            src_ref=own.at[pl.ds(pl.multiple_of(j * rows, rows), rows)],
+            dst_ref=rs.at[slot if to_me else chip],
+            send_sem=rs_send.at[i], recv_sem=rs_recv.at[i],
+            device_id={"tensor": j * 2 + c},
+        )
+
+    @pl.loop(1, CHIPS)
+    def _(i):
+        scatter(i, False).start()
+
+    rs[chip] = own[pl.ds(pl.multiple_of(chip * rows, rows), rows)]
+
+    @pl.loop(1, CHIPS)
+    def _(i):
+        scatter(i, True).wait_recv()
+
+    def place(ch, cc):
+        return pl.ds(pl.multiple_of((cc * CHIPS + ch) * rows, rows), rows)
+
+    out_ref[place(chip, c)] = jnp.sum(rs[...], axis=0)
+
+    def spread(i, to_me):
+        j = (chip + i) % CHIPS
+        src = (chip + CHIPS - i) % CHIPS
+        return pltpu.make_async_remote_copy(
+            src_ref=out_ref.at[place(chip, c)],
+            dst_ref=out_ref.at[place(src if to_me else chip, c)],
+            send_sem=ag_send.at[i], recv_sem=ag_recv.at[i],
+            device_id={"tensor": j * 2 + c},
+        )
+
+    def across(i, cc):
+        src = (chip + CHIPS - i) % CHIPS
+        return pltpu.make_async_remote_copy(
+            src_ref=out_ref.at[place(src, cc)], dst_ref=out_ref.at[place(src, cc)],
+            send_sem=sib_send.at[i], recv_sem=sib_recv.at[i], device_id={"tensor": sib},
+        )
+
+    @pl.loop(1, CHIPS)
+    def _(i):
+        spread(i, False).start()
+
+    across(0, c).start()
+
+    @pl.loop(1, CHIPS)
+    def _(i):
+        spread(i, True).wait_recv()
+        across(i, c).start()
+
+    @pl.loop(0, CHIPS)
+    def _(i):
+        across(i, 1 - c).wait_recv()
+
+    for a, h, owner, to, slot, cond in pending:
+        if cond is None:
+            copy(a, h, owner, to, slot).wait_send()
+        else:
+            @pl.when(cond)
+            def _(a=a, h=h, owner=owner, to=to, slot=slot):
+                copy(a, h, owner, to, slot).wait_send()
+    swap.wait_send()
+
+    @pl.loop(1, CHIPS)
+    def _(i):
+        scatter(i, False).wait_send()
+        spread(i, False).wait_send()
+
+    @pl.loop(0, CHIPS)
+    def _(i):
+        across(i, c).wait_send()
+
+
+N_SEND = 2 * 2 * (5 + 3 * 4 + 4 * 2 + 8)
+
+
+def fused_sides(
+    layer_input, out_grad, norm_gain, w_gate, w_up, w_down,
+    pin_gate, pin_up, pout_gate, pout_up, pin_down, pout_down,
+):
+    tokens, width = layer_input.shape
+    hid, d = w_gate.shape[1], w_gate.shape[0]
+    rank = pin_gate.shape[1]
+    vmem = pl.BlockSpec(memory_space=pltpu.VMEM)
+    hbm = pl.BlockSpec(memory_space=pl.ANY)
+    dma = pltpu.SemaphoreType.DMA
+    return pl.pallas_call(
+        kernel,
+        out_shape=jax.ShapeDtypeStruct((tokens, 6 * rank), F32),
+        in_specs=[vmem, vmem, vmem, hbm, hbm, hbm] + [vmem] * 6,
+        out_specs=vmem,
+        scratch_shapes=[
+            pltpu.VMEM((2, 32, tokens, width), BF16),
+            pltpu.VMEM((2 * PAD, d), BF16),
+            pltpu.VMEM((hid, d), BF16),
+            pltpu.VMEM((tokens, 128), F32),
+            pltpu.VMEM((tokens, 2 * PAD), F32),
+            pltpu.VMEM((tokens, hid), F32),
+            pltpu.VMEM((tokens, 6 * rank), F32),
+            pltpu.VMEM((tokens // 2, 6 * rank), F32),
+            pltpu.VMEM((tokens // 2, 6 * rank), F32),
+            pltpu.VMEM((CHIPS, tokens // 2 // CHIPS, 6 * rank), F32),
+            dma((128,)), dma((N_SEND,)), dma((3,)), dma((2,)),
+            dma((CHIPS,)), dma((CHIPS,)), dma((CHIPS,)), dma((CHIPS,)), dma((CHIPS,)), dma((CHIPS,)),
+        ],
+        compiler_params=pltpu.CompilerParams(
+            collective_id=0, has_side_effects=True, vmem_limit_bytes=40 * 1024 * 1024
+        ),
+        cost_estimate=pl.CostEstimate(
+            flops=6 * tokens * d * hid, bytes_accessed=6 * d * hid, transcendentals=tokens * hid
+        ),
+    )(
+        layer_input, out_grad, norm_gain.reshape(1, -1), w_gate.T, w_up.T, w_down,
+        pin_gate.T, pin_up.T, pout_gate.T, pout_up.T, pin_down.T, pout_down.T,
+    )
+
+
+def on_device_fused(*args):
+    targets = args[-1]
+    sides = fused_sides(*args[:-1])
+    rank = sides.shape[1] // 6
+    a_gate, a_up, b_down, b_gate, b_up, a_down = (
+        sides[:, i * rank:(i + 1) * rank] for i in range(6)
+    )
+    features = jnp.concatenate(
+        [project_pair(b_gate, a_gate), project_pair(b_up, a_up), project_pair(b_down, a_down)],
+        axis=1,
+    )
+    scores = jnp.dot(
+        features, targets.T, precision=lax.Precision.HIGHEST, preferred_element_type=jnp.float32
+    )
+    return (features, scores)
 
 
 def project_pair(out_side, in_side):
@@ -82,8 +436,9 @@
 
 
 def solution(mesh):
+    fused = mesh.shape["tensor"] == 2 * CHIPS and mesh.shape["dp"] == 1 and mesh.shape["groups"] == 1
     return jax.shard_map(
-        on_device,
+        on_device_fused if fused else on_device,
         mesh=mesh,
         in_specs=(
             P(("groups", "dp"), "tensor"),

time: 316 us -> 86.7 us (0.27)
  waiting for transfers between devices: 261 us -> 0 us
  Pallas kernels: 0 us -> 70.1 us
  matrix products: 23 us -> 3.07 us
  between operations: 13.9 us -> 0.72 us
  other arithmetic: 4.45 us -> 0 us
    all_gather x2 -> x0, waiting for transfers between devices: 130 us -> none  [the longest x1 69.4 us: on_device(): gathered = lax.all_gather(layer_input, 'tensor', axis=1, tiled=True)]
    psum x1 -> x0, waiting for transfers between devices: 129 us -> none  [on_device(): lax.psum((a_gate_part, a_up_part, b_down_part, b_gate_part, b_up_part, a_...]
    pallas_call x0 -> x1, Pallas kernels: none -> 70.1 us  [fused_sides(): pl.pallas_call(kernel, out_shape=jax.ShapeDtypeStruct((tokens, 6 * rank),...]
    dot_general x7 -> x1, matrix products: 15 us -> 1.91 us  [on_device_fused(): jnp.dot(features, targets.T, precision=lax.Precision.HIGHEST, preferred_e...]
    unnamed x22 -> x30, local copies, waits for them, and re-layouts: 5.75 us -> 11.6 us
    reshape x3 -> x0, matrix products: 4.35 us -> none  [project_pair(): in_rows = in_side.reshape(-1, SEQ, in_side.shape[-1])]
    reduce_sum x1 -> x0, other arithmetic: 3.25 us -> none  [on_device(): mean_square = jnp.mean(wide_rows * wide_rows, axis=-1, keepdims=True)]
    reshape x6 -> x0, local copies, waits for them, and re-layouts: 3.19 us -> none  [project_pair(): out_rows = out_side.reshape(-1, SEQ, out_side.shape[-1])]
  transfers between devices with their start and end apart: 3 -> 0, of which waited for: 3 -> 0; matrix products, arithmetic and copies ran while one was open for 2% -> 0% of each run, Pallas kernels for 0% -> 0%
where the time goes in v1:
time: 86.7 us; the launch traced here: 86.1 us
  Pallas kernels  70.1 us (81%)
  local copies, waits for them, and re-layouts  12.2 us (14%)
  matrix products  3.07 us (4%)
    pallas_call x1, Pallas kernels, fused_sides(): pl.pallas_call(kernel, out_shape=jax.ShapeDtypeStruct((tokens, 6 * rank),...  70.1 us
    unnamed x30, local copies, waits for them, and re-layouts  11.6 us
    dot_general x1, matrix products, on_device_fused(): jnp.dot(features, targets.T, precision=lax.Precision.HIGHEST, preferred_e...  1.91 us

profile of v1, /device:TPU:1, one launch (start us, length us, event | category | flops | bytes accessed | tf_op | source)
XLA Modules:
  0.0 86.1 jit_solution(8235150455818860823)
XLA Ops:
  0.6 0.0 copy-start
  0.7 0.0 copy-start.1
  0.7 1.6 %copy-done.1 = bf16[8192,112]{0,1:T(8,128)(2,1)S(1)} copy-done((bf16[8192,112]{0,1:T(8,128)(2,1)S(1)}, bf16[8192,112]{0,1:T(8,128)(2,1)}, u32[]{:S(2)}) %copy-start.1) | copy-done | bytes 1835032
  2.3 0.0 copy-start.2
  2.3 1.5 %copy-done.2 = bf16[8192,112]{0,1:T(8,128)(2,1)S(1)} copy-done((bf16[8192,112]{0,1:T(8,128)(2,1)S(1)}, bf16[8192,112]{0,1:T(8,128)(2,1)}, u32[]{:S(2)}) %copy-start.2) | copy-done | bytes 1835032
  3.8 0.0 copy-start.3
  3.8 1.5 %copy-done.3 = bf16[112,8192]{1,0:T(8,128)(2,1)S(1)} copy-done((bf16[112,8192]{1,0:T(8,128)(2,1)S(1)}, bf16[112,8192]{1,0:T(8,128)(2,1)}, u32[]{:S(2)}) %copy-start.3) | copy-done | bytes 1835032
  5.3 0.0 copy-start.4
  5.3 0.9 %copy-done.4 = bf16[256,256]{1,0:T(8,128)(2,1)S(1)} copy-done((bf16[256,256]{1,0:T(8,128)(2,1)S(1)}, bf16[256,256]{1,0:T(8,128)(2,1)}, u32[]{:S(2)}) %copy-start.4) | copy-done | bytes 131096
  6.2 0.0 copy-start.5
  6.2 0.9 %copy-done.5 = bf16[256,256]{1,0:T(8,128)(2,1)S(1)} copy-done((bf16[256,256]{1,0:T(8,128)(2,1)S(1)}, bf16[256,256]{1,0:T(8,128)(2,1)}, u32[]{:S(2)}) %copy-start.5) | copy-done | bytes 131096
  7.1 0.0 copy-start.6
  7.1 0.8 copy-done.6
  7.8 0.0 copy-start.7
  7.8 0.8 copy-done.7
  8.6 0.0 copy-start.8
  8.6 0.8 copy-done.8
  9.4 0.0 copy-start.9
  9.4 0.8 copy-done.9
  10.1 0.0 copy-start.10
  10.1 0.7 copy-done.10
  10.8 0.0 copy-start.11
  10.8 0.7 copy-done.11
  11.5 0.0 copy-start.12
  11.6 0.7 copy-done.12
  12.3 70.1 %shard_map.140 = f32[256,384]{1,0:T(8,128)S(1)} custom-call(bf16[256,256]{1,0:T(8,128)(2,1)S(1)} %copy-done.4, bf16[256,256]{1,0:T(8,128)(2,1)S(1)} %copy-done.5, f32[1,8192]{1,0:T(1,128)S(1)} %bitcast.25, bf16[112,8192]{1,0:T(8,128)(2,1)S(1)} %bitcast.23, bf16[112,8192]{1,0:T(8,128)(2,1)S(1)} %bitcast.24, bf16[112,8192]{1,0:T(8,128)(2,1)S(1)} %copy-done.3, ...), custom_call_target="tpu_custom_call" | custom-call | flops 1409286144 | bytes 5505024 | tf_op jit(solution)/shard_map/pallas_call | solution.py:318
  82.4 0.2 fusion
  82.6 0.4 fusion.3
  83.0 0.1 reshape.43
  83.1 0.4 fusion.2
  83.5 0.1 reshape.40
  83.6 0.4 fusion.1
  84.0 0.1 reshape.37
  84.1 0.0 copy-done
  84.1 0.0 copy-start.13
  84.2 1.9 %fusion.4 = f32[4,32]{1,0:T(4,128)} fusion(f32[4,12288]{1,0:T(4,128)S(1)} %constant_dynamic-update-slice_fusion, f32[32,12288]{1,0:T(8,128)S(1)} %copy-done), kind=kOutput, calls=%fused_computation.7 | convolution fusion | flops 18874368 | bytes 1769984 | tf_op jit(solution)/shard_map/dot_general | solution.py:360
  86.1 0.0 copy-done.13
  (3 shorter events, 0.0 us)
Async XLA Ops:
  0.6 83.5 %copy-start = (f32[32,12288]{1,0:T(8,128)S(1)}, f32[32,12288]{1,0:T(8,128)}, u32[]{:S(2)}) copy-start(f32[32,12288]{1,0:T(8,128)} %param.25) | copy-start | bytes 4718596
  0.7 1.6 %copy-start.1 = (bf16[8192,112]{0,1:T(8,128)(2,1)S(1)}, bf16[8192,112]{0,1:T(8,128)(2,1)}, u32[]{:S(2)}) copy-start(bf16[8192,112]{0,1:T(8,128)(2,1)} %param.16) | copy-start | bytes 5505028
  2.3 1.5 %copy-start.2 = (bf16[8192,112]{0,1:T(8,128)(2,1)S(1)}, bf16[8192,112]{0,1:T(8,128)(2,1)}, u32[]{:S(2)}) copy-start(bf16[8192,112]{0,1:T(8,128)(2,1)} %param.17) | copy-start | bytes 5505028
  3.8 1.5 %copy-start.3 = (bf16[112,8192]{1,0:T(8,128)(2,1)S(1)}, bf16[112,8192]{1,0:T(8,128)(2,1)}, u32[]{:S(2)}) copy-start(bf16[112,8192]{1,0:T(8,128)(2,1)} %wd_hbm.1) | copy-start | bytes 5505028
  5.3 0.9 %copy-start.4 = (bf16[256,256]{1,0:T(8,128)(2,1)S(1)}, bf16[256,256]{1,0:T(8,128)(2,1)}, u32[]{:S(2)}) copy-start(bf16[256,256]{1,0:T(8,128)(2,1)} %x_ref.1) | copy-start | bytes 393220
  6.2 0.9 %copy-start.5 = (bf16[256,256]{1,0:T(8,128)(2,1)S(1)}, bf16[256,256]{1,0:T(8,128)(2,1)}, u32[]{:S(2)}) copy-start(bf16[256,256]{1,0:T(8,128)(2,1)} %g_ref.1) | copy-start | bytes 393220
  7.1 0.8 copy-start.6
  7.8 0.8 copy-start.7
  8.6 0.8 copy-start.8
  9.4 0.8 copy-start.9
  10.1 0.7 copy-start.10
  10.8 0.7 copy-start.11
  11.5 0.7 copy-start.12
  84.1 1.9 %copy-start.13 = (f32[4,12288]{1,0:T(4,128)}, f32[4,12288]{1,0:T(4,128)S(1)}, u32[]{:S(2)}) copy-start(f32[4,12288]{1,0:T(4,128)S(1)} %constant_dynamic-update-slice_fusion) | copy-start | bytes 589828

commit v2 on v1

--- a/solution.py
+++ b/solution.py
@@ -21,24 +21,37 @@
 
 
 def kernel(
-    x_ref, g_ref, gain_ref, wg_hbm, wu_hbm, wd_hbm, pg_ref, pu_ref, qg_ref, qu_ref, pd_ref, qd_ref,
-    out_ref,
-    buf, wgu, wd, ss, gu_acc, h_acc, part, pair, own, rs,
-    recv, send, w_sem, pair_sem, rs_send, rs_recv, ag_send, ag_recv, sib_send, sib_recv,
+    x_hbm, g_hbm, gain_hbm, wg_hbm, wu_hbm, wd_hbm, pg_hbm, pu_hbm, qg_hbm, qu_hbm, pd_hbm, qd_hbm,
+    oute_ref, outl_ref,
+    buf, wgu, wd, gate_factor, up_factor, gain_ref, pg_ref, pu_ref, qg_ref, qu_ref, pd_ref, qd_ref,
+    ss, gu_acc, h_acc, part_e, pair_e, own_e, rs_e, part_l, pair_l, own_l, rs_l,
+    recv, send, w_sem, pair_send, pair_recv, rs_send, rs_recv, ag_send, ag_recv, sib_send, sib_recv,
 ):
     me = lax.axis_index("tensor")
     z, y, x, c = me // 8, (me // 4) % 2, (me // 2) % 2, me % 2
     chip = me // 2
     sib = me + 1 - 2 * c
-    width = x_ref.shape[1]
-    tokens = x_ref.shape[0]
+    tokens, width = x_hbm.shape
     half = tokens // 2
     hid = wg_hbm.shape[0]
 
+    mine_in = [
+        pltpu.make_async_copy(x_hbm, buf.at[0, me], w_sem.at[10]),
+        pltpu.make_async_copy(g_hbm, buf.at[1, me], w_sem.at[11]),
+    ]
+    for load in mine_in:
+        load.start()
     loads = [
         pltpu.make_async_copy(wg_hbm, wgu.at[pl.ds(0, hid)], w_sem.at[0]),
         pltpu.make_async_copy(wu_hbm, wgu.at[pl.ds(PAD, hid)], w_sem.at[1]),
         pltpu.make_async_copy(wd_hbm, wd, w_sem.at[2]),
+        pltpu.make_async_copy(gain_hbm, gain_ref, w_sem.at[3]),
+        pltpu.make_async_copy(pg_hbm, pg_ref, w_sem.at[4]),
+        pltpu.make_async_copy(pu_hbm, pu_ref, w_sem.at[5]),
+        pltpu.make_async_copy(qg_hbm, qg_ref, w_sem.at[6]),
+        pltpu.make_async_copy(qu_hbm, qu_ref, w_sem.at[7]),
+        pltpu.make_async_copy(pd_hbm, pd_ref, w_sem.at[8]),
+        pltpu.make_async_copy(qd_hbm, qd_ref, w_sem.at[9]),
     ]
     for load in loads:
         load.start()
@@ -51,8 +64,8 @@
         pl.semaphore_signal(barrier, inc=1, device_id={"tensor": peer})
 
     pl.semaphore_signal(barrier, inc=1, device_id={"tensor": sib})
-    buf[0, me] = x_ref[...]
-    buf[1, me] = g_ref[...]
+    for load in mine_in:
+        load.wait()
     pl.semaphore_wait(barrier, CHIPS)
 
     def dev(zz, fy, fx, cc):
@@ -106,20 +119,16 @@
                     arrive(a, h, owner)
                 n1 = dev(z, 0, 1, c) if h == 0 else dev(z, 1, 0, c)
                 n2 = dev(z, 1, 0, c) if h == 0 else dev(z, 0, 1, c)
-                if stage == 0:
+                if stage == 0 or (stage == 1 and a == 1):
                     if k == 0:
                         start(a, h, owner, me + 8, z < 3)
                         start(a, h, owner, me - 8, z > 0)
-                    elif k < 3:
-                        up = order[k] < z
-                        start(a, h, owner, jnp.where(up, me + 8, me - 8),
-                              jnp.logical_or(jnp.logical_and(up, z < 3),
-                                             jnp.logical_and(order[k] > z, z > 0)))
                     else:
                         up = order[k] < z
                         start(a, h, owner, jnp.where(up, me + 8, me - 8),
                               jnp.logical_or(jnp.logical_and(up, z < 3),
                                              jnp.logical_and(order[k] > z, z > 0)))
+                if stage == 0 and (a == 0 or k == 0):
                     start(a, h, owner, n1)
                 if stage < 2:
                     start(a, h, owner, n2)
@@ -141,19 +150,23 @@
             v = v * v
             ss[...] += v[:, :128] + v[:, 128:]
 
+    def grad_block(owner):
+        cols = pl.ds(pl.multiple_of(owner * width, width), width)
+        h_acc[...] += dot_nt(buf[1, owner], wd[:, cols])
+
     def grads(k, cc):
         @pl.loop(0, 4)
         def _(i):
-            owner = owner_of(k, i, cc)
-            cols = pl.ds(pl.multiple_of(owner * width, width), width)
-            h_acc[...] += dot_nt(buf[1, owner], wd[:, cols])
-
-    def tick(a, t):
+            grad_block(owner_of(k, i, cc))
+
+    def tick(a, t, between=None):
         work = squares if a == 0 else grads
         for stage in (0, 1, 2):
             k = t - stage
             if 0 <= k < 4:
                 lane_event(a, stage, k)
+                if between is not None:
+                    between()
         k = t - 2
         if 0 <= k < 4:
             work(k, c)
@@ -192,97 +205,127 @@
     total = jnp.sum(ss[...], axis=1, keepdims=True)
     ss[...] = jnp.broadcast_to(lax.rsqrt(total / (32 * width) + EPSILON), ss.shape)
     rank = pg_ref.shape[0]
-    tick(1, 3)
-    pre(0, 12)
-    tick(1, 4)
-    pre(12, 24)
-    tick(1, 5)
-    pre(24, 32)
+    done = [0]
+
+    def some_pre(n=7):
+        pre(done[0], min(done[0] + n, 32))
+        done[0] = min(done[0] + n, 32)
+
+    rows = half // CHIPS
+    GROUPS = ((part_e, pair_e, own_e, rs_e, oute_ref), (part_l, pair_l, own_l, rs_l, outl_ref))
+
+    def swap(g):
+        part, pair = GROUPS[g][0], GROUPS[g][1]
+        return pltpu.make_async_remote_copy(
+            src_ref=part.at[pl.ds(pl.multiple_of((1 - c) * half, half), half)], dst_ref=pair,
+            send_sem=pair_send.at[g], recv_sem=pair_recv.at[g], device_id={"tensor": sib},
+        )
+
+    def scatter(g, i, to_me):
+        own, rs = GROUPS[g][2], GROUPS[g][3]
+        j = (chip + i) % CHIPS
+        slot = (chip + CHIPS - i) % CHIPS
+        return pltpu.make_async_remote_copy(
+            src_ref=own.at[pl.ds(pl.multiple_of(j * rows, rows), rows)],
+            dst_ref=rs.at[slot if to_me else chip],
+            send_sem=rs_send.at[g * CHIPS + i], recv_sem=rs_recv.at[g * CHIPS + i],
+            device_id={"tensor": j * 2 + c},
+        )
+
+    def place(ch, cc):
+        return pl.ds(pl.multiple_of((cc * CHIPS + ch) * rows, rows), rows)
+
+    def spread(g, i, to_me):
+        out = GROUPS[g][4]
+        j = (chip + i) % CHIPS
+        src = (chip + CHIPS - i) % CHIPS
+        return pltpu.make_async_remote_copy(
+            src_ref=out.at[place(chip, c)],
+            dst_ref=out.at[place(src if to_me else chip, c)],
+            send_sem=ag_send.at[g * CHIPS + i], recv_sem=ag_recv.at[g * CHIPS + i],
+            device_id={"tensor": j * 2 + c},
+        )
+
+    def across(g, cc):
+        block = GROUPS[g][4].at[pl.ds(pl.multiple_of(cc * half, half), half)]
+        return pltpu.make_async_remote_copy(
+            src_ref=block, dst_ref=block, send_sem=sib_send.at[g], recv_sem=sib_recv.at[g],
+            device_id={"tensor": sib},
+        )
+
+    def start_scatter(g):
+        part, pair, own, rs, _ = GROUPS[g]
+        swap(g).wait_recv()
+        own[...] = part[pl.ds(pl.multiple_of(c * half, half), half)] + pair[...]
+
+        @pl.loop(1, CHIPS)
+        def _(i):
+            scatter(g, i, False).start()
+
+        rs[chip] = own[pl.ds(pl.multiple_of(chip * rows, rows), rows)]
+
+    def start_spread(g):
+        @pl.loop(1, CHIPS)
+        def _(i):
+            scatter(g, i, True).wait_recv()
+
+        GROUPS[g][4][place(chip, c)] = jnp.sum(GROUPS[g][3][...], axis=0)
+
+        @pl.loop(1, CHIPS)
+        def _(i):
+            spread(g, i, False).start()
+
+    def relay(g):
+        @pl.loop(1, CHIPS)
+        def _(i):
+            spread(g, i, True).wait_recv()
+
+        across(g, c).start()
+
+    def finish(g):
+        across(g, 1 - c).wait_recv()
+
+    def drain(g):
+        swap(g).wait_send()
+
+        @pl.loop(1, CHIPS)
+        def _(i):
+            scatter(g, i, False).wait_send()
+            spread(g, i, False).wait_send()
+
+        across(g, c).wait_send()
+
+    tick(1, 3, some_pre)
+    some_pre(11)
     mine, _ = normed_of(me)
-    part[:, 0:rank] = dot_nt(mine, pg_ref[...])
-    part[:, rank:2 * rank] = dot_nt(mine, pu_ref[...])
-    part[:, 2 * rank:3 * rank] = dot_nt(g_ref[...], qd_ref[...])
+    part_e[:, 0:rank] = dot_nt(mine, pg_ref[...])
+    part_e[:, rank:2 * rank] = dot_nt(mine, pu_ref[...])
+    part_e[:, 2 * rank:3 * rank] = dot_nt(buf[1, me], qd_ref[...])
     gate_pre = gu_acc[:, 0:hid]
     up_pre = gu_acc[:, PAD:PAD + hid]
     sigmoid_gate = jax.nn.sigmoid(gate_pre)
     activated = gate_pre * sigmoid_gate
     hidden_act = (activated * up_pre).astype(BF16)
-    part[:, 5 * rank:6 * rank] = dot_nt(hidden_act, pd_ref[...])
-    tick(1, 6)
+    part_e[:, 3 * rank:4 * rank] = dot_nt(hidden_act, pd_ref[...])
+    swap(0).start()
+    gate_factor[...] = up_pre * sigmoid_gate * (1.0 + gate_pre * (1.0 - sigmoid_gate))
+    up_factor[...] = activated
+    tick(1, 4)
+    start_scatter(0)
+    tick(1, 5)
+    start_spread(0)
+    for i in range(4):
+        for h in (0, 1):
+            arrive(1, h, owner_of(3, i, 1 - c))
+        grad_block(owner_of(3, i, 1 - c))
     grad_hidden = h_acc[...]
-    grad_gate = (
-        grad_hidden * up_pre * sigmoid_gate * (1.0 + gate_pre * (1.0 - sigmoid_gate))
-    ).astype(BF16)
-    grad_up = (grad_hidden * activated).astype(BF16)
-    part[:, 3 * rank:4 * rank] = dot_nt(grad_gate, qg_ref[...])
-    part[:, 4 * rank:5 * rank] = dot_nt(grad_up, qu_ref[...])
-
-    swap = pltpu.make_async_remote_copy(
-        src_ref=part.at[pl.ds(pl.multiple_of((1 - c) * half, half), half)], dst_ref=pair,
-        send_sem=pair_sem.at[0], recv_sem=pair_sem.at[1], device_id={"tensor": sib},
-    )
-    swap.start()
-    rows = half // CHIPS
-    swap.wait_recv()
-    own[...] = part[pl.ds(pl.multiple_of(c * half, half), half)] + pair[...]
-
-    def scatter(i, to_me):
-        j = (chip + i) % CHIPS
-        slot = (chip + CHIPS - i) % CHIPS
-        return pltpu.make_async_remote_copy(
-            src_ref=own.at[pl.ds(pl.multiple_of(j * rows, rows), rows)],
-            dst_ref=rs.at[slot if to_me else chip],
-            send_sem=rs_send.at[i], recv_sem=rs_recv.at[i],
-            device_id={"tensor": j * 2 + c},
-        )
-
-    @pl.loop(1, CHIPS)
-    def _(i):
-        scatter(i, False).start()
-
-    rs[chip] = own[pl.ds(pl.multiple_of(chip * rows, rows), rows)]
-
-    @pl.loop(1, CHIPS)
-    def _(i):
-        scatter(i, True).wait_recv()
-
-    def place(ch, cc):
-        return pl.ds(pl.multiple_of((cc * CHIPS + ch) * rows, rows), rows)
-
-    out_ref[place(chip, c)] = jnp.sum(rs[...], axis=0)
-
-    def spread(i, to_me):
-        j = (chip + i) % CHIPS
-        src = (chip + CHIPS - i) % CHIPS
-        return pltpu.make_async_remote_copy(
-            src_ref=out_ref.at[place(chip, c)],
-            dst_ref=out_ref.at[place(src if to_me else chip, c)],
-            send_sem=ag_send.at[i], recv_sem=ag_recv.at[i],
-            device_id={"tensor": j * 2 + c},
-        )
-
-    def across(i, cc):
-        src = (chip + CHIPS - i) % CHIPS
-        return pltpu.make_async_remote_copy(
-            src_ref=out_ref.at[place(src, cc)], dst_ref=out_ref.at[place(src, cc)],
-            send_sem=sib_send.at[i], recv_sem=sib_recv.at[i], device_id={"tensor": sib},
-        )
-
-    @pl.loop(1, CHIPS)
-    def _(i):
-        spread(i, False).start()
-
-    across(0, c).start()
-
-    @pl.loop(1, CHIPS)
-    def _(i):
-        spread(i, True).wait_recv()
-        across(i, c).start()
-
-    @pl.loop(0, CHIPS)
-    def _(i):
-        across(i, 1 - c).wait_recv()
-
+    grad_gate = (grad_hidden * gate_factor[...]).astype(BF16)
+    grad_up = (grad_hidden * up_factor[...]).astype(BF16)
+    part_l[:, 0:rank] = dot_nt(grad_gate, qg_ref[...])
+    part_l[:, rank:2 * rank] = dot_nt(grad_up, qu_ref[...])
+    swap(1).start()
+    start_scatter(1)
+    relay(0)
     for a, h, owner, to, slot, cond in pending:
         if cond is None:
             copy(a, h, owner, to, slot).wait_send()
@@ -290,19 +333,15 @@
             @pl.when(cond)
             def _(a=a, h=h, owner=owner, to=to, slot=slot):
                 copy(a, h, owner, to, slot).wait_send()
-    swap.wait_send()
-
-    @pl.loop(1, CHIPS)
-    def _(i):
-        scatter(i, False).wait_send()
-        spread(i, False).wait_send()
-
-    @pl.loop(0, CHIPS)
-    def _(i):
-        across(i, c).wait_send()
-
-
-N_SEND = 2 * 2 * (5 + 3 * 4 + 4 * 2 + 8)
+    start_spread(1)
+    relay(1)
+    finish(0)
+    finish(1)
+    drain(0)
+    drain(1)
+
+
+N_SEND = 2 * (33 + 35)
 
 
 def fused_sides(
@@ -317,25 +356,41 @@
     dma = pltpu.SemaphoreType.DMA
     return pl.pallas_call(
         kernel,
-        out_shape=jax.ShapeDtypeStruct((tokens, 6 * rank), F32),
-        in_specs=[vmem, vmem, vmem, hbm, hbm, hbm] + [vmem] * 6,
-        out_specs=vmem,
+        out_shape=[
+            jax.ShapeDtypeStruct((tokens, 4 * rank), F32),
+            jax.ShapeDtypeStruct((tokens, 2 * rank), F32),
+        ],
+        in_specs=[hbm] * 12,
+        out_specs=[vmem, vmem],
         scratch_shapes=[
             pltpu.VMEM((2, 32, tokens, width), BF16),
             pltpu.VMEM((2 * PAD, d), BF16),
             pltpu.VMEM((hid, d), BF16),
+            pltpu.VMEM((tokens, hid), F32),
+            pltpu.VMEM((tokens, hid), F32),
+            pltpu.VMEM((1, d), F32),
+            pltpu.VMEM((rank, width), BF16),
+            pltpu.VMEM((rank, width), BF16),
+            pltpu.VMEM((rank, hid), BF16),
+            pltpu.VMEM((rank, hid), BF16),
+            pltpu.VMEM((rank, hid), BF16),
+            pltpu.VMEM((rank, width), BF16),
             pltpu.VMEM((tokens, 128), F32),
             pltpu.VMEM((tokens, 2 * PAD), F32),
             pltpu.VMEM((tokens, hid), F32),
-            pltpu.VMEM((tokens, 6 * rank), F32),
-            pltpu.VMEM((tokens // 2, 6 * rank), F32),
-            pltpu.VMEM((tokens // 2, 6 * rank), F32),
-            pltpu.VMEM((CHIPS, tokens // 2 // CHIPS, 6 * rank), F32),
-            dma((128,)), dma((N_SEND,)), dma((3,)), dma((2,)),
-            dma((CHIPS,)), dma((CHIPS,)), dma((CHIPS,)), dma((CHIPS,)), dma((CHIPS,)), dma((CHIPS,)),
+            pltpu.VMEM((tokens, 4 * rank), F32),
+            pltpu.VMEM((tokens // 2, 4 * rank), F32),
+            pltpu.VMEM((tokens // 2, 4 * rank), F32),
+            pltpu.VMEM((CHIPS, tokens // 2 // CHIPS, 4 * rank), F32),
+            pltpu.VMEM((tokens, 2 * rank), F32),
+            pltpu.VMEM((tokens // 2, 2 * rank), F32),
+            pltpu.VMEM((tokens // 2, 2 * rank), F32),
+            pltpu.VMEM((CHIPS, tokens // 2 // CHIPS, 2 * rank), F32),
+            dma((128,)), dma((N_SEND,)), dma((12,)), dma((2,)), dma((2,)),
+        ] + [dma((2 * CHIPS,))] * 4 + [dma((2,))] * 2 + [
         ],
         compiler_params=pltpu.CompilerParams(
-            collective_id=0, has_side_effects=True, vmem_limit_bytes=40 * 1024 * 1024
+            collective_id=0, has_side_effects=True, vmem_limit_bytes=60 * 1024 * 1024
         ),
         cost_estimate=pl.CostEstimate(
             flops=6 * tokens * d * hid, bytes_accessed=6 * d * hid, transcendentals=tokens * hid
@@ -348,11 +403,10 @@
 
 def on_device_fused(*args):
     targets = args[-1]
-    sides = fused_sides(*args[:-1])
-    rank = sides.shape[1] // 6
-    a_gate, a_up, b_down, b_gate, b_up, a_down = (
-        sides[:, i * rank:(i + 1) * rank] for i in range(6)
-    )
+    early, late = fused_sides(*args[:-1])
+    rank = late.shape[1] // 2
+    a_gate, a_up, b_down, a_down = (early[:, i * rank:(i + 1) * rank] for i in range(4))
+    b_gate, b_up = late[:, :rank], late[:, rank:]
     features = jnp.concatenate(
         [project_pair(b_gate, a_gate), project_pair(b_up, a_up), project_pair(b_down, a_down)],
         axis=1,

time: 86.7 us -> 75.8 us (0.87)
  local copies, waits for them, and re-layouts: 12.2 us -> 1.75 us
    unnamed x30 -> x6, local copies, waits for them, and re-layouts: 11.6 us -> 0.04 us
    slice x1, local copies, waits for them, and re-layouts: 0.18 us -> 1.37 us  [on_device_fused(): early[:, i * rank:(i + 1) * rank]]
where the time goes in v2:
time: 75.8 us; the launch traced here: 75.7 us
  Pallas kernels  70.2 us (93%)
  matrix products  3.07 us (4%)
  local copies, waits for them, and re-layouts  1.75 us (2%)
    pallas_call x1, Pallas kernels, fused_sides(): pl.pallas_call(kernel, out_shape=[jax.ShapeDtypeStruct((tokens, 4 * rank)...  70.2 us
    dot_general x1, matrix products, on_device_fused(): jnp.dot(features, targets.T, precision=lax.Precision.HIGHEST, preferred_e...  1.91 us

profile of v2, /device:TPU:1, one launch (start us, length us, event | category | flops | bytes accessed | tf_op | source)
XLA Modules:
  0.0 75.7 jit_solution(16592727077152631613)
XLA Ops:
  0.6 0.0 copy-start
  0.7 70.2 %shard_map.140 = (f32[256,256]{1,0:T(8,128)}, f32[256,128]{1,0:T(8,128)}) custom-call(bf16[256,256]{1,0:T(8,128)(2,1)} %x_hbm.1, bf16[256,256]{1,0:T(8,128)(2,1)} %g_hbm.1, f32[1,8192]{1,0:T(1,128)} %bitcast.31, bf16[112,8192]{1,0:T(8,128)(2,1)} %bitcast.23, bf16[112,8192]{1,0:T(8,128)(2,1)} %bitcast.24, bf16[112,8192]{1,0:T(8,128)(2,1)} %wd_hbm.1, ...), custom_call_target="tpu_custom_call" | custom-call | flops 1409286144 | bytes 5505024 | tf_op jit(solution)/shard_map/pallas_call | solution.py:357
  70.8 1.4 %fusion = (f32[256,64]{1,0:T(8,128)S(1)}, f32[256,64]{1,0:T(8,128)S(1)}, f32[256,64]{1,0:T(8,128)S(1)}, f32[256,64]{1,0:T(8,128)S(1)}, f32[256,64]{1,0:T(8,128)S(1)}, /*index=5*/f32[256,64]{1,0:T(8,128)S(1)}) fusion(f32[256,256]{1,0:T(8,128)} %get-tuple-element.5, f32[256,128]{1,0:T(8,128)} %get-tuple-element.4), kind=kLoop, calls=%fused_computation.3 | loop fusion | bytes 786432 | tf_op jit(solution)/shard_map/slice | solution.py:408
  72.2 0.4 fusion.4
  72.6 0.1 reshape.43
  72.7 0.4 fusion.3
  73.1 0.1 reshape.40
  73.2 0.4 fusion.2
  73.6 0.1 reshape.37
  73.7 0.0 copy-done
  73.7 0.0 copy-start.1
  73.8 1.9 %fusion.5 = f32[4,32]{1,0:T(4,128)} fusion(f32[4,12288]{1,0:T(4,128)S(1)} %constant_dynamic-update-slice_fusion, f32[32,12288]{1,0:T(8,128)S(1)} %copy-done), kind=kOutput, calls=%fused_computation.8 | convolution fusion | flops 18874368 | bytes 1769984 | tf_op jit(solution)/shard_map/dot_general | solution.py:414
  75.7 0.0 copy-done.1
  (3 shorter events, 0.0 us)
Async XLA Ops:
  0.6 73.1 %copy-start = (f32[32,12288]{1,0:T(8,128)S(1)}, f32[32,12288]{1,0:T(8,128)}, u32[]{:S(2)}) copy-start(f32[32,12288]{1,0:T(8,128)} %param.25) | copy-start | bytes 4718596
  73.7 1.9 %copy-start.1 = (f32[4,12288]{1,0:T(4,128)}, f32[4,12288]{1,0:T(4,128)S(1)}, u32[]{:S(2)}) copy-start(f32[4,12288]{1,0:T(4,128)S(1)} %constant_dynamic-update-slice_fusion) | copy-start | bytes 589828

commit v3 on v2

--- a/solution.py
+++ b/solution.py
@@ -119,7 +119,7 @@
                     arrive(a, h, owner)
                 n1 = dev(z, 0, 1, c) if h == 0 else dev(z, 1, 0, c)
                 n2 = dev(z, 1, 0, c) if h == 0 else dev(z, 0, 1, c)
-                if stage == 0 or (stage == 1 and a == 1):
+                if stage == 0 or (stage == 1 and a == 0):
                     if k == 0:
                         start(a, h, owner, me + 8, z < 3)
                         start(a, h, owner, me - 8, z > 0)
@@ -128,7 +128,7 @@
                         start(a, h, owner, jnp.where(up, me + 8, me - 8),
                               jnp.logical_or(jnp.logical_and(up, z < 3),
                                              jnp.logical_and(order[k] > z, z > 0)))
-                if stage == 0 and (a == 0 or k == 0):
+                if stage == 0 and (a == 1 or k == 0):
                     start(a, h, owner, n1)
                 if stage < 2:
                     start(a, h, owner, n2)
@@ -150,14 +150,13 @@
             v = v * v
             ss[...] += v[:, :128] + v[:, 128:]
 
-    def grad_block(owner):
+    def grad_term(owner):
         cols = pl.ds(pl.multiple_of(owner * width, width), width)
-        h_acc[...] += dot_nt(buf[1, owner], wd[:, cols])
+        return dot_nt(buf[1, owner], wd[:, cols])
 
     def grads(k, cc):
-        @pl.loop(0, 4)
-        def _(i):
-            grad_block(owner_of(k, i, cc))
+        terms = [grad_term(owner_of(k, i, cc)) for i in range(4)]
+        h_acc[...] += (terms[0] + terms[1]) + (terms[2] + terms[3])
 
     def tick(a, t, between=None):
         work = squares if a == 0 else grads
@@ -181,10 +180,11 @@
         return (buf[0, owner].astype(F32) * scale * gain_ref[:, cols]).astype(BF16), cols
 
     def pre(lo, hi):
-        @pl.loop(lo, hi)
-        def _(owner):
-            normed, cols = normed_of(owner)
-            gu_acc[...] += dot_nt(normed, wgu[:, cols])
+        @pl.loop(lo // 2, hi // 2)
+        def _(pair):
+            first, cols = normed_of(pair * 2)
+            second, next_cols = normed_of(pair * 2 + 1)
+            gu_acc[...] += dot_nt(first, wgu[:, cols]) + dot_nt(second, wgu[:, next_cols])
 
     ss[...] = jnp.zeros_like(ss)
     gu_acc[...] = jnp.zeros_like(gu_acc)
@@ -207,7 +207,7 @@
     rank = pg_ref.shape[0]
     done = [0]
 
-    def some_pre(n=7):
+    def some_pre(n=8):
         pre(done[0], min(done[0] + n, 32))
         done[0] = min(done[0] + n, 32)
 
@@ -296,7 +296,7 @@
         across(g, c).wait_send()
 
     tick(1, 3, some_pre)
-    some_pre(11)
+    some_pre()
     mine, _ = normed_of(me)
     part_e[:, 0:rank] = dot_nt(mine, pg_ref[...])
     part_e[:, rank:2 * rank] = dot_nt(mine, pu_ref[...])
@@ -317,7 +317,7 @@
     for i in range(4):
         for h in (0, 1):
             arrive(1, h, owner_of(3, i, 1 - c))
-        grad_block(owner_of(3, i, 1 - c))
+        h_acc[...] += grad_term(owner_of(3, i, 1 - c))
     grad_hidden = h_acc[...]
     grad_gate = (grad_hidden * gate_factor[...]).astype(BF16)
     grad_up = (grad_hidden * up_factor[...]).astype(BF16)

time: 75.8 us -> 73.2 us (0.966)
  Pallas kernels: 70.2 us -> 67.5 us
    pallas_call x1, Pallas kernels: 70.2 us -> 67.5 us  [fused_sides(): pl.pallas_call(kernel, out_shape=[jax.ShapeDtypeStruct((tokens, 4 * rank)...]
where the time goes in v3:
time: 73.2 us; the launch traced here: 73 us
  Pallas kernels  67.5 us (92%)
  matrix products  3.07 us (4%)
  local copies, waits for them, and re-layouts  1.75 us (2%)
    pallas_call x1, Pallas kernels, fused_sides(): pl.pallas_call(kernel, out_shape=[jax.ShapeDtypeStruct((tokens, 4 * rank)...  67.5 us
    dot_general x1, matrix products, on_device_fused(): jnp.dot(features, targets.T, precision=lax.Precision.HIGHEST, preferred_e...  1.91 us

profile of v3, /device:TPU:1, one launch (start us, length us, event | category | flops | bytes accessed | tf_op | source)
XLA Modules:
  0.0 73.0 jit_solution(1541151965835747531)
XLA Ops:
  0.6 0.0 copy-start
  0.7 67.5 %shard_map.140 = (f32[256,256]{1,0:T(8,128)}, f32[256,128]{1,0:T(8,128)}) custom-call(bf16[256,256]{1,0:T(8,128)(2,1)} %x_hbm.1, bf16[256,256]{1,0:T(8,128)(2,1)} %g_hbm.1, f32[1,8192]{1,0:T(1,128)} %bitcast.31, bf16[112,8192]{1,0:T(8,128)(2,1)} %bitcast.23, bf16[112,8192]{1,0:T(8,128)(2,1)} %bitcast.24, bf16[112,8192]{1,0:T(8,128)(2,1)} %wd_hbm.1, ...), custom_call_target="tpu_custom_call" | custom-call | flops 1409286144 | bytes 5505024 | tf_op jit(solution)/shard_map/pallas_call | solution.py:357
  68.2 1.4 %fusion = (f32[256,64]{1,0:T(8,128)S(1)}, f32[256,64]{1,0:T(8,128)S(1)}, f32[256,64]{1,0:T(8,128)S(1)}, f32[256,64]{1,0:T(8,128)S(1)}, f32[256,64]{1,0:T(8,128)S(1)}, /*index=5*/f32[256,64]{1,0:T(8,128)S(1)}) fusion(f32[256,256]{1,0:T(8,128)} %get-tuple-element.5, f32[256,128]{1,0:T(8,128)} %get-tuple-element.4), kind=kLoop, calls=%fused_computation.3 | loop fusion | bytes 786432 | tf_op jit(solution)/shard_map/slice | solution.py:408
  69.5 0.4 fusion.4
  69.9 0.1 reshape.43
  70.0 0.4 fusion.3
  70.4 0.1 reshape.40
  70.5 0.4 fusion.2
  70.9 0.1 reshape.37
  71.1 0.0 copy-done
  71.1 0.0 copy-start.1
  71.1 1.9 %fusion.5 = f32[4,32]{1,0:T(4,128)} fusion(f32[4,12288]{1,0:T(4,128)S(1)} %constant_dynamic-update-slice_fusion, f32[32,12288]{1,0:T(8,128)S(1)} %copy-done), kind=kOutput, calls=%fused_computation.8 | convolution fusion | flops 18874368 | bytes 1769984 | tf_op jit(solution)/shard_map/dot_general | solution.py:414
  73.0 0.0 copy-done.1
  (3 shorter events, 0.0 us)
Async XLA Ops:
  0.6 70.5 %copy-start = (f32[32,12288]{1,0:T(8,128)S(1)}, f32[32,12288]{1,0:T(8,128)}, u32[]{:S(2)}) copy-start(f32[32,12288]{1,0:T(8,128)} %param.25) | copy-start | bytes 4718596
  71.1 1.9 %copy-start.1 = (f32[4,12288]{1,0:T(4,128)}, f32[4,12288]{1,0:T(4,128)S(1)}, u32[]{:S(2)}) copy-start(f32[4,12288]{1,0:T(4,128)S(1)} %constant_dynamic-update-slice_fusion) | copy-start | bytes 589828
